TPU v7x, 32 devices: a whole 2x2x4 slice. The times are simulated.
32 devices in a mesh: sky: 4 (over z), tile: 8 (over y, x, core).
Axes of the slice: x: 2, y: 2, z: 4, core: 2. Of those that a mesh axis runs over, the one named last changes fastest.
Arguments:
- science: float32 [4, 8, 2, 128, 512], P('sky', 'tile'), may hold values from -6 to 6
- inverse_variance: bfloat16 [4, 8, 2, 128, 512], P('sky', 'tile'), may hold values from 0.25 to 4
- template: bfloat16 [4, 8, 128, 512], P('sky', 'tile'), may hold values from -6 to 6
- filters: bfloat16 [8, 21], replicated, may hold values from -1.25 to 1.25
- kernel_index: int32 [20, 2], replicated, may hold values from 0 to 7
- spatial_coeff: float32 [4, 8, 2, 3, 20], P('sky', 'tile'), may hold values from -1.5 to 1.5
- visit_offset: int32 [4, 2], P('sky'), may hold values from 0 to 7
- block_count: int32 [4, 8, 2], P('sky', 'tile'), may hold values from 12 to 16, as said below
- block_owner: int32 [4, 8, 32], P('sky', 'tile'), may hold values from 0 to 7, as said below
- block_slot: int32 [4, 8, 32], P('sky', 'tile'), may hold values from 0 to 2
- coadd_sum: float32 [4, 8, 3, 4096], P('sky', 'tile'), may hold values from -18 to 18
- coadd_weight: float32 [4, 8, 3, 4096], P('sky', 'tile'), may hold values from 2 to 8
Outputs:
- difference: float32 [4, 8, 2, 128, 512], P('sky', 'tile')
- coadd: float32 [4, 8, 3, 4096], P('sky', 'tile')
Inputs may be any that keep to these rules, and one draw needn't show every extreme that they name: `visit_offset`: exposure tile i of a group lies in visit v on template tile (i + offset) mod 8. `block_count`: blocks 0 to count - 1 of a tile and visit enter the coadd. `block_owner`: among the 32 blocks of one device no owner appears more than 6 times; in each sky group one owner receives exactly 6 blocks from every device of the group, their first 6 blocks.
All inputs are finite; a program needn't handle non-finite values.
Results may differ from a plain program's by a relative error of at most 0.0026.
Values may be sent and summed in bfloat16 or wider, within the bound.
A program may use at most 64 MiB of HBM per device.

v0:
```python
import jax
import jax.numpy as jnp
from jax import lax
from jax.sharding import PartitionSpec as P

BS = 64


def with_halo(cells, sides, width):
    for axis, dim in sides:
        count = lax.axis_size(axis)
        ends = count - 1
        head = lax.slice_in_dim(cells, 0, width, axis=dim)
        tail = lax.slice_in_dim(cells, cells.shape[dim] - width, cells.shape[dim], axis=dim)
        cells = jnp.concatenate(
            [
                lax.ppermute(tail, axis, [(i, (i + 1) % count) for i in range(ends)]),
                cells,
                lax.ppermute(head, axis, [((i + 1) % count, i) for i in range(ends)]),
            ],
            axis=dim,
        )
    return cells


def block_rows(image):
    visits, height, tile_width = image.shape
    pieces = image.reshape(visits, height // BS, BS, tile_width // BS, BS)
    return jnp.transpose(pieces, (0, 1, 3, 2, 4)).reshape(-1, BS * BS)


def shards(
    science,
    inverse_variance,
    template,
    filters,
    kernel_index,
    spatial_coeff,
    visit_offset,
    block_count,
    block_owner,
    block_slot,
    coadd_sum,
    coadd_weight,
):
    tile_count = lax.axis_size("tile")
    own_tile = template[0, 0]
    height, tile_width = own_tile.shape
    visits = science.shape[2]
    offsets = visit_offset[0]
    strips = own_tile.reshape(tile_count, height // tile_count, tile_width)
    held_strips = lax.all_to_all(strips, "tile", split_axis=0, concat_axis=0, tiled=True)
    outgoing = jnp.stack([jnp.roll(held_strips, -offsets[v], axis=0) for v in range(visits)])
    arrived = lax.all_to_all(outgoing, "tile", split_axis=1, concat_axis=1, tiled=True)
    aligned = arrived.reshape(visits, height, tile_width)
    basis_count, tap_total = filters.shape
    half_width = tap_total // 2
    kernel_total = kernel_index.shape[0]
    taps_all = filters.astype(jnp.float32)
    block_width = min(128, tile_width)
    block_total = tile_width // block_width
    window_width = block_width + 2 * half_width
    window_pos = lax.broadcasted_iota(jnp.int32, (window_width, block_width), 0)
    output_pos = lax.broadcasted_iota(jnp.int32, (window_width, block_width), 1)
    tap_offset = window_pos - output_pos
    band_table = jnp.zeros((window_width, basis_count, block_width), jnp.float32)
    for q in range(tap_total):
        band_table = band_table + jnp.where(
            (tap_offset == q)[:, None, :], taps_all[None, :, q, None], 0.0
        )
    band_table = band_table.astype(jnp.bfloat16)
    padded = jnp.pad(
        aligned.reshape(visits * height, tile_width), ((0, 0), (half_width, half_width))
    )
    windows = jnp.stack(
        [padded[:, b * block_width : b * block_width + window_width] for b in range(block_total)],
        axis=1,
    )
    filtered = jnp.einsum("rbq,qjx->rjbx", windows, band_table, preferred_element_type=jnp.float32)
    filtered = filtered.astype(jnp.bfloat16).reshape(visits, height, basis_count, tile_width)
    basis_ids = jnp.arange(basis_count, dtype=jnp.int32)
    row_pick = (kernel_index[:, 0, None] == basis_ids[None, :]).astype(jnp.bfloat16)
    column_pick = (kernel_index[:, 1, None] == basis_ids[None, :]).astype(jnp.float32)
    column_taps = jnp.dot(
        column_pick, taps_all, precision=lax.Precision.HIGHEST, preferred_element_type=jnp.float32
    )
    target_row = lax.broadcasted_iota(jnp.int32, (height, height), 0)
    source_row = lax.broadcasted_iota(jnp.int32, (height, height), 1)
    row_offset = source_row - target_row + half_width
    column_band = jnp.zeros((kernel_total, height, height), jnp.float32)
    for p in range(tap_total):
        column_band = column_band + jnp.where(
            (row_offset == p)[None, :, :], column_taps[:, p, None, None], 0.0
        )
    across = (2.0 * jnp.arange(tile_width, dtype=jnp.float32) + 1.0 - tile_width) / tile_width
    downward = (2.0 * jnp.arange(height, dtype=jnp.float32) + 1.0 - height) / height
    band_stack = jnp.concatenate([column_band, downward[None, :, None] * column_band], axis=0)
    selected = jnp.einsum("kj,vhjw->vkhw", row_pick, filtered, preferred_element_type=jnp.float32)
    coeffs = spatial_coeff[0, 0]
    column_weight = coeffs[:, 0, :, None] + coeffs[:, 1, :, None] * across[None, None, :]
    operand_stack = jnp.concatenate(
        [selected * column_weight[:, :, None, :], selected * coeffs[:, 2, :, None, None]], axis=1
    )
    matched = jnp.einsum(
        "kyg,vkgw->vyw",
        band_stack,
        operand_stack,
        precision=lax.Precision.HIGHEST,
        preferred_element_type=jnp.float32,
    )
    difference = science[0, 0] - matched
    inverse = inverse_variance[0, 0].astype(jnp.float32)
    blocks_per_visit = height // BS * (tile_width // BS)
    row_total = visits * blocks_per_visit
    weighted = block_rows(inverse * difference)
    weight_rows = block_rows(inverse)
    row_index = jnp.arange(row_total, dtype=jnp.int32)
    limits = jnp.repeat(block_count[0, 0], blocks_per_visit)
    is_valid = row_index % blocks_per_visit < limits
    row_mask = is_valid.astype(jnp.float32)
    payload = jnp.concatenate([weighted, weight_rows], axis=1) * row_mask[:, None]
    owners = block_owner[0, 0]
    patch_slot = block_slot[0, 0]
    patch_count = coadd_sum.shape[2]
    destination = owners * patch_count + patch_slot
    wanted = lax.broadcasted_iota(jnp.int32, (patch_count * lax.axis_size("tile"), row_total), 0)
    picker = (wanted == destination[None, :]).astype(jnp.float32)
    patches = lax.psum_scatter(
        jnp.dot(
            picker, payload, precision=lax.Precision.HIGHEST, preferred_element_type=jnp.float32
        ),
        "tile",
        scatter_dimension=0,
        tiled=True,
    )
    stacked = patches.reshape(patch_count, 2, -1)
    widened = with_halo(stacked, (("sky", 0),), 1)
    merged = stacked.at[0].add(widened[0]).at[-1].add(widened[-1])
    result = (coadd_sum[0, 0] + merged[:, 0]) / (coadd_weight[0, 0] + merged[:, 1])
    return (difference[None, None], result[None, None])


def solution(mesh):
    return jax.shard_map(
        shards,
        mesh=mesh,
        in_specs=(
            P("sky", "tile", None, None, None),
            P("sky", "tile", None, None, None),
            P("sky", "tile", None, None),
            P(),
            P(),
            P("sky", "tile", None, None, None),
            P("sky", None),
            P("sky", "tile", None),
            P("sky", "tile", None),
            P("sky", "tile", None),
            P("sky", "tile", None, None),
            P("sky", "tile", None, None),
        ),
        out_specs=(P("sky", "tile", None, None, None), P("sky", "tile", None, None)),
        check_vma=False,
    )
```

profile of v0, /device:TPU:0, one launch (start us, length us, event | category | flops | bytes accessed | tf_op | source)
XLA Modules:
  0.0 175.2 jit_solution(11497324686275384520)
XLA Ops:
  7.2 5.2 %all-to-all-start = ((bf16[8,16,512]{2,1,0:T(8,128)(2,1)}), bf16[8,16,512]{2,1,0:T(8,128)(2,1)S(1)}, u32[]{:S(2)}, u32[]{:S(2)}) async-start(bf16[8,16,512]{2,1,0:T(8,128)(2,1)} %bitcast.112), calls=%async_computation | async-start | bytes 262144 | tf_op jit(solution)/shard_map/all_to_all | solution.py:52
  12.6 0.6 fusion.83
  13.2 0.6 fusion.85
  13.9 0.7 fusion.87
  15.1 0.7 convert_element_type.34
  15.8 1.3 slice_bitcast_fusion.8
  17.1 0.9 fusion.115
  19.1 1.4 fusion.126
  21.1 0.8 slice_reduce_fusion.40
  21.9 1.3 slice_bitcast_fusion.6
  23.2 0.7 broadcast_in_dim.749
  24.5 1.3 add_bitcast_fusion
  25.8 6.2 %broadcast_multiply_fusion = (f32[20,128,128]{1,0,2:T(8,128)}, f32[20,128,128]{1,0,2:T(8,128)}) fusion(f32[128]{0:T(128)S(1)} %add_multiply_fusion.1, f32[20]{0:T(128)S(1)} %get-tuple-element.36, pred[128,128]{0,1:T(8,128)(4,1)S(1)} %get-tuple-element.96, f32[20]{0:T(128)S(1)} %get-tuple-element.37, pred[128,128]{0,1:T(8,128)(4,1)S(1)} %get-tuple-element.97, ...), kind=kLoop, calls=%fused_computation.16 | loop fusion | flops 13762560 | bytes 2967696 | tf_op jit(solution)/shard_map/mul | solution.py:97
  32.8 1.0 slice_reduce_fusion.41
  33.9 0.7 pad_maximum_fusion
  34.6 4.2 %all-to-all-start.1 = ((bf16[2,8,16,512]{3,2,0,1:T(8,128)(2,1)}), bf16[2,8,16,512]{3,2,0,1:T(8,128)(2,1)S(1)}, u32[]{:S(2)}, u32[]{:S(2)}) async-start(bf16[2,8,16,512]{3,2,0,1:T(8,128)(2,1)} %pad_maximum_fusion), calls=%async_computation.1 | async-start | bytes 524288 | tf_op jit(solution)/shard_map/all_to_all | solution.py:54
  39.8 1.0 copy.35
  42.7 3.0 %all-to-all-done.1 = bf16[2,8,16,512]{3,2,0,1:T(8,128)(2,1)S(1)} async-done(((bf16[2,8,16,512]{3,2,0,1:T(8,128)(2,1)}), bf16[2,8,16,512]{3,2,0,1:T(8,128)(2,1)S(1)}, u32[]{:S(2)}, u32[]{:S(2)}) %all-to-all-start.1) | async-done | bytes 262176 | tf_op jit(solution)/shard_map/all_to_all | solution.py:54
  46.0 3.1 %convert_bitcast_fusion = bf16[256,8,4,128]{0,3,2,1:T(8,128)(2,1)S(1)} fusion(bf16[256,1,148]{0,2,1:T(8,128)(2,1)S(1)} %get-tuple-element.82, bf16[256,1,148]{0,2,1:T(8,128)(2,1)S(1)} %get-tuple-element.83, bf16[256,1,148]{0,2,1:T(8,128)(2,1)S(1)} %get-tuple-element.84, bf16[256,1,148]{0,2,1:T(8,128)(2,1)S(1)} %get-tuple-element.81, ...), kind=kOutput, calls=%fused_computation.9 | convolution fusion | flops 319004672 | bytes 2798752 | tf_op jit(solution)/shard_map/rbq,qjx->rjbx/dot_general | solution.py:79
  49.1 2.1 %reshape.406 = bf16[2,128,8,512]{1,0,3,2:T(2,128)(2,1)} reshape(bf16[256,8,4,128]{0,3,2,1:T(8,128)(2,1)S(1)} %convert_bitcast_fusion) | data formatting | bytes 4194304 | tf_op jit(solution)/shard_map/reshape | solution.py:80
  51.2 3.6 %copy.40 = bf16[2,128,8,512]{3,2,1,0:T(8,128)(2,1)S(1)} copy(bf16[2,128,8,512]{1,0,3,2:T(2,128)(2,1)} %reshape.406) | data formatting | bytes 4194304 | tf_op jit(solution)/shard_map/reshape | solution.py:80
  54.8 6.5 %bitcast_multiply_fusion.1 = (f32[2,20,128,512]{3,1,2,0:T(8,128)S(1)}, f32[2,20,128,512]{3,1,2,0:T(8,128)}) fusion(f32[2,20,512]{2,1,0:T(8,128)S(1)} %multiply_add_fusion, f32[2,20]{1,0:T(2,128)S(1)} %get-tuple-element.88, bf16[2,128,8,512]{3,2,1,0:T(8,128)(2,1)S(1)} %copy.40, s32[20]{0:T(128)S(1)} %copy-done.10), kind=kOutput, calls=%fused_computation.5 | convolution fusion | flops 47186080 | bytes 23150832 | tf_op jit(solution)/shard_map/kj,vhjw->vkhw/dot_general | solution.py:98
  61.3 36.5 %bitcast_multiply_fusion.2 = (f32[2,128,512]{1,2,0:T(8,128)S(1)}, f32[2,128,512]{1,2,0:T(8,128)S(1)}) fusion(bf16[1,1,2,128,512]{3,4,2,1,0:T(8,128)(2,1)S(1)} %copy.41, f32[20,128,128]{1,0,2:T(8,128)S(1)} %copy-done, f32[20,128,128]{1,0,2:T(8,128)S(1)} %copy-done.1, f32[2,20,128,512]{3,1,2,0:T(8,128)} %get-tuple-element.80, ...), kind=kOutput, calls=%fused_computation.19 | convolution fusion | flops 8059355136 | bytes 25427968 | tf_op jit(solution)/shard_map/kyg,vkgw->vyw/dot_general | solution.py:104
  99.4 1.5 fusion.9
  102.2 1.0 copy.46
  103.2 52.8 %all-reduce.4.cloned.1.call-done = f32[24,8192]{1,0:T(8,128)} async-done(((f32[24,8192]{1,0:T(8,128)}), f32[24,8192]{1,0:T(8,128)}) %all-reduce.4.cloned.1.call-update) | async-done | bytes 786448
  156.0 1.2 dynamic-slice_reduce_fusion
  157.3 3.2 %collective-permute-start = (f32[1,2,4096]{2,1,0:T(2,128)S(1)}, f32[1,2,4096]{2,1,0:T(2,128)S(1)}, u32[]{:S(2)}, u32[]{:S(2)}) collective-permute-start(f32[1,2,4096]{2,1,0:T(2,128)S(1)} %slice.277), channel_id=1, source_target_pairs={{0,8},{8,16},{16,24},{1,9},{9,17},{17,25},{2,10},{10,18},{18,26},{... | collective-permute-start | bytes 98312 | tf_op jit(solution)/shard_map/ppermute | solution.py:17
  160.5 1.1 constant_dynamic-slice_fusion
  161.7 1.3 collective-permute-start.1
  163.1 4.5 %collective-permute-done.1 = f32[1,2,4096]{2,1,0:T(2,128)S(1)} collective-permute-done((f32[1,2,4096]{2,1,0:T(2,128)S(1)}, f32[1,2,4096]{2,1,0:T(2,128)S(1)}, u32[]{:S(2)}, u32[]{:S(2)}) %collective-permute-start.1) | collective-permute-done | bytes 32800 | tf_op jit(solution)/shard_map/ppermute | solution.py:19
  167.6 0.7 fusion.112
  (77 shorter events, 7.9 us)
Async XLA Ops:
  7.2 26.7 %all-to-all-start = ((bf16[8,16,512]{2,1,0:T(8,128)(2,1)}), bf16[8,16,512]{2,1,0:T(8,128)(2,1)S(1)}, u32[]{:S(2)}, u32[]{:S(2)}) async-start(bf16[8,16,512]{2,1,0:T(8,128)(2,1)} %bitcast.112), calls=%async_computation | async-start | bytes 262144 | tf_op jit(solution)/shard_map/all_to_all | solution.py:52
  32.0 7.7 %copy-start.4 = (bf16[1,1,2,128,512]{4,3,2,1,0:T(8,128)(2,1)S(1)}, bf16[1,1,2,128,512]{4,3,2,1,0:T(8,128)(2,1)}, u32[]{:S(2)}) copy-start(bf16[1,1,2,128,512]{4,3,2,1,0:T(8,128)(2,1)} %param.19) | copy-start | bytes 786436
  32.0 7.8 %copy-start.2 = (f32[1,1,2,128,512]{4,3,2,1,0:T(8,128)S(1)}, f32[1,1,2,128,512]{4,3,2,1,0:T(8,128)}, u32[]{:S(2)}) copy-start(f32[1,1,2,128,512]{4,3,2,1,0:T(8,128)} %param.18) | copy-start | bytes 1572868
  34.6 11.1 %all-to-all-start.1 = ((bf16[2,8,16,512]{3,2,0,1:T(8,128)(2,1)}), bf16[2,8,16,512]{3,2,0,1:T(8,128)(2,1)S(1)}, u32[]{:S(2)}, u32[]{:S(2)}) async-start(bf16[2,8,16,512]{3,2,0,1:T(8,128)(2,1)} %pad_maximum_fusion), calls=%async_computation.1 | async-start | bytes 524288 | tf_op jit(solution)/shard_map/all_to_all | solution.py:54
  38.8 117.2 %all-reduce.4.cloned.1.call-start = ((), (), s32[]{:S(2)}) async-start(), calls=%async_computation.2 | async-start | bytes 1572864
  42.0 0.7 copy-start.7
  42.0 0.7 copy-start.8
  42.0 0.7 copy-start.9
  51.2 3.6 %copy-start.10 = (s32[20]{0:T(128)S(1)}, s32[20]{0:T(128)}, u32[]{:S(2)}) copy-start(s32[20]{0:T(128)} %get-tuple-element.90) | copy-start | bytes 244
  54.7 6.5 %copy-start = (f32[20,128,128]{1,0,2:T(8,128)S(1)}, f32[20,128,128]{1,0,2:T(8,128)}, u32[]{:S(2)}) copy-start(f32[20,128,128]{1,0,2:T(8,128)} %get-tuple-element.77) | copy-start | bytes 3932164
  54.7 6.5 %copy-start.1 = (f32[20,128,128]{1,0,2:T(8,128)S(1)}, f32[20,128,128]{1,0,2:T(8,128)}, u32[]{:S(2)}) copy-start(f32[20,128,128]{1,0,2:T(8,128)} %get-tuple-element.78) | copy-start | bytes 3932164
  54.8 6.5 %copy-start.3 = (f32[1,1,2,128,512]{3,4,2,1,0:T(8,128)S(1)}, f32[1,1,2,128,512]{3,4,2,1,0:T(8,128)}, u32[]{:S(2)}) copy-start(f32[1,1,2,128,512]{3,4,2,1,0:T(8,128)} %copy.35) | copy-start | bytes 1572868
  98.5 0.9 copy-start.11
  98.5 0.9 copy-start.12
  99.4 1.6 copy-start.13
  100.9 66.7 %copy-start.5 = (f32[1,1,3,4096]{3,1,2,0:T(1,128)S(1)}, f32[1,1,3,4096]{3,1,2,0:T(1,128)}, u32[]{:S(2)}) copy-start(f32[1,1,3,4096]{3,1,2,0:T(1,128)} %param.29) | copy-start | bytes 147460
  100.9 66.7 %copy-start.6 = (f32[1,1,3,4096]{3,1,2,0:T(1,128)S(1)}, f32[1,1,3,4096]{3,1,2,0:T(1,128)}, u32[]{:S(2)}) copy-start(f32[1,1,3,4096]{3,1,2,0:T(1,128)} %param.28) | copy-start | bytes 147460
  157.3 5.8 %collective-permute-start = (f32[1,2,4096]{2,1,0:T(2,128)S(1)}, f32[1,2,4096]{2,1,0:T(2,128)S(1)}, u32[]{:S(2)}, u32[]{:S(2)}) collective-permute-start(f32[1,2,4096]{2,1,0:T(2,128)S(1)} %slice.277), channel_id=1, source_target_pairs={{0,8},{8,16},{16,24},{1,9},{9,17},{17,25},{2,10},{10,18},{18,26},{... | collective-permute-start | bytes 98312 | tf_op jit(solution)/shard_map/ppermute | solution.py:17
  161.7 5.8 %collective-permute-start.1 = (f32[1,2,4096]{2,1,0:T(2,128)S(1)}, f32[1,2,4096]{2,1,0:T(2,128)S(1)}, u32[]{:S(2)}, u32[]{:S(2)}) collective-permute-start(f32[1,2,4096]{2,1,0:T(2,128)S(1)} %reshape.413), channel_id=1, source_target_pairs={{8,0},{16,8},{24,16},{9,1},{17,9},{25,17},{10,2},{18,10},{26,18},{... | collective-permute-start | bytes 98312 | tf_op jit(solution)/shard_map/ppermute | solution.py:19
Sparse Core Ops, SparseCore 0:
  101.1 54.9 all-reduce.3
where the time goes:
time: 176 us; the launch traced here: 175 us
  waiting for transfers between devices  60.3 us (34%)
  matrix products  48.5 us (28%)
  local copies, waits for them, and re-layouts  21.7 us (12%)
  between operations  16.6 us (9%)
  starting transfers between devices  14.1 us (8%)
  other arithmetic  13.9 us (8%)
    unnamed x2, waiting for transfers between devices  52.8 us
    dot_general x1, matrix products, shards(): jnp.einsum('kyg,vkgw->vyw', band_stack, operand_stack, precision=lax.Prec...  36.5 us
    dot_general x1, matrix products, shards(): jnp.einsum('kj,vhjw->vkhw', row_pick, filtered, preferred_element_type=jn...  6.51 us
    mul x1, other arithmetic, shards(): downward[None, :, None] * column_band  6.19 us
    reshape x2, local copies, waits for them, and re-layouts, shards(): filtered.astype(jnp.bfloat16)  5.65 us
    all_to_all x1, starting transfers between devices, shards(): lax.all_to_all(strips, 'tile', split_axis=0, concat_axis=0, tiled=True)  5.18 us
    ppermute x1, waiting for transfers between devices, with_halo(): lax.ppermute(head, axis, [((i + 1) % count, i) for i in range(ends)])  4.47 us
    all_to_all x1, starting transfers between devices, shards(): lax.all_to_all(outgoing, 'tile', split_axis=1, concat_axis=1, tiled=True)  4.2 us
  transfers between devices with their start and end apart: 5, of which 3 were waited for; matrix products, arithmetic and copies ran while one was open for 15% of the time, Pallas kernels for 0%

commit v1 on v0

v1 whole, which is shorter than its diff:
```python
import functools

import jax
import jax.numpy as jnp
from jax import lax
from jax.experimental import pallas as pl
from jax.experimental.pallas import tpu as pltpu
from jax.sharding import PartitionSpec as P

BS = 64
LANES = 128
MESH = pl.DeviceIdType.MESH
F32 = jnp.float32
BF16 = jnp.bfloat16


def greet(peers):
    barrier = pltpu.get_barrier_semaphore()
    for peer in peers:
        pl.semaphore_signal(barrier, inc=1, device_id=peer, device_id_type=MESH)
    return barrier


def align_kernel(n, visits, offset_ref, template_ref, out_ref, own, held, outgoing, send1, recv1, send2, recv2):
    sky = lax.axis_index("sky")
    me = lax.axis_index("tile")
    peers = [lax.rem(me + k, n) for k in range(1, n)]
    barrier = greet([(sky, peer) for peer in peers])
    height, width = template_ref.shape[-2:]
    tiles = width // LANES
    strip = height * tiles // n
    for t in range(tiles):
        own[t * height : (t + 1) * height, :] = template_ref[0, 0, :, t * LANES : (t + 1) * LANES]
    pl.semaphore_wait(barrier, n - 1)
    first = []
    for k, peer in enumerate(peers):
        copy = pltpu.make_async_remote_copy(
            src_ref=own.at[pl.ds(pl.multiple_of(peer * strip, strip), strip)],
            dst_ref=held.at[me],
            send_sem=send1.at[k],
            recv_sem=recv1.at[k],
            device_id=(sky, peer),
            device_id_type=MESH,
        )
        copy.start()
        first.append(copy)
    held[me] = own[pl.ds(pl.multiple_of(me * strip, strip), strip), :]
    for copy in first:
        copy.wait_recv()
    second = []
    for k, peer in enumerate(peers):
        for v in range(visits):
            place = peer + offset_ref[0, v]
            place = jnp.where(place >= n, place - n, place)
            outgoing[k, v] = held[place]
        copy = pltpu.make_async_remote_copy(
            src_ref=outgoing.at[k],
            dst_ref=out_ref.at[me],
            send_sem=send2.at[k],
            recv_sem=recv2.at[k],
            device_id=(sky, peer),
            device_id_type=MESH,
        )
        copy.start()
        second.append(copy)
    for v in range(visits):
        place = me + offset_ref[0, v]
        place = jnp.where(place >= n, place - n, place)
        out_ref[me, v] = held[place]
    for copy in first:
        copy.wait_send()
    for copy in second:
        copy.wait()


def toeplitz(rows):
    return pltpu.roll(rows, 0, 1, stride=1, stride_axis=0)


def match_kernel(
    patch_total,
    patches,
    strips_ref,
    filters_ref,
    index_ref,
    coeff_ref,
    science_ref,
    inverse_ref,
    count_ref,
    owner_ref,
    slot_ref,
    diff_ref,
    pay_ref,
    filtered,
    row_band,
    band_high,
    band_low,
    image,
    total,
):
    n, visits, strip, lanes = strips_ref.shape
    height, width = science_ref.shape[-2:]
    tiles = width // LANES
    basis, taps = filters_ref.shape
    half = taps // 2
    kernels = index_ref.shape[0]

    tap_id = lax.broadcasted_iota(jnp.int32, (taps, LANES), 0)
    lane_id = lax.broadcasted_iota(jnp.int32, (taps, LANES), 1)
    spread_row = (lane_id == lax.rem(half - tap_id + LANES, LANES)).astype(BF16)
    spread_col = (lane_id == lax.rem(tap_id - half + LANES, LANES)).astype(BF16)
    filters = filters_ref[...]
    row_taps = jnp.dot(filters, spread_row, preferred_element_type=F32)
    col_taps = jnp.dot(filters, spread_col, preferred_element_type=F32).astype(BF16)

    y = lax.broadcasted_iota(jnp.int32, (height, LANES), 0)
    x = lax.broadcasted_iota(jnp.int32, (height, LANES), 1)
    gap = y - x
    near = jnp.abs(gap) <= half
    before = gap >= LANES - half
    after = gap <= half - LANES
    for j in range(basis):
        full = toeplitz(jnp.broadcast_to(row_taps[j : j + 1, :], (LANES, LANES)))
        span = slice(j * LANES, (j + 1) * LANES)
        row_band[0:LANES, span] = jnp.where(before, full, 0.0).astype(BF16)
        row_band[LANES : 2 * LANES, span] = jnp.where(near, full, 0.0).astype(BF16)
        row_band[2 * LANES : 3 * LANES, span] = jnp.where(after, full, 0.0).astype(BF16)

    index = index_ref[...]
    basis_id = lax.broadcasted_iota(jnp.int32, (kernels, basis), 1)
    pick_col = (index[:, 1:2] == basis_id).astype(BF16)
    kernel_taps = jnp.dot(pick_col, col_taps, preferred_element_type=F32)
    spread = jnp.concatenate(
        [jnp.where(index[:, 0:1] == j, kernel_taps, 0.0) for j in range(basis)], axis=1
    )
    downward = (2.0 * y.astype(F32) + (1.0 - height)) / height
    for v in range(visits):
        mixed = jnp.dot(
            coeff_ref[0, 0, v], spread, precision=lax.Precision.HIGHEST, preferred_element_type=F32
        )
        for j in range(basis):
            span = slice(j * LANES, (j + 1) * LANES)
            steady = mixed[0:1, span] + downward * mixed[2:3, span]
            across = jnp.broadcast_to(mixed[1:2, span], (height, LANES))
            for part, rows in enumerate((steady, across)):
                band = jnp.where(near, toeplitz(rows), 0.0)
                high = band.astype(BF16)
                down = slice(part * height, (part + 1) * height)
                band_high[v, down, span] = high
                band_low[v, down, span] = (band - high.astype(F32)).astype(BF16)

    per_tile = height // strip if strip <= height else 1
    source = []
    for t in range(tiles):
        rows = []
        for v in range(visits):
            rows += [strips_ref[t * per_tile + s, v] for s in range(per_tile)]
        source.append(jnp.concatenate(rows, axis=0))
    for t in range(tiles):
        low, top = max(t - 1, 0), min(t + 2, tiles)
        window = jnp.concatenate(source[low:top], axis=1)
        band = row_band[(low - t + 1) * LANES : (top - t + 1) * LANES, :]
        out = jnp.dot(window, band, preferred_element_type=F32).astype(BF16)
        for v in range(visits):
            for j in range(basis):
                filtered[v, j * height : (j + 1) * height, t * LANES : (t + 1) * LANES] = out[
                    v * height : (v + 1) * height, j * LANES : (j + 1) * LANES
                ]

    total[...] = jnp.zeros_like(total)
    x_id = lax.broadcasted_iota(jnp.int32, (1, width), 1).astype(F32)
    rightward = (2.0 * x_id + (1.0 - width)) / width
    low_lanes = lax.broadcasted_iota(jnp.int32, (BS // 2, LANES), 1) < BS
    downs = height // BS
    blocks = downs * (width // BS)
    for v in range(visits):
        operand = filtered[v]
        product = jnp.dot(band_high[v], operand, preferred_element_type=F32) + jnp.dot(
            band_low[v], operand, preferred_element_type=F32
        )
        difference = science_ref[0, 0, v] - (product[:height] + rightward * product[height:])
        diff_ref[0, 0, v] = difference
        inverse = inverse_ref[0, 0, v].astype(F32)
        weighted = inverse * difference
        for t in range(tiles):
            image[0, t] = weighted[:, t * LANES : (t + 1) * LANES]
            image[1, t] = inverse[:, t * LANES : (t + 1) * LANES]
        limit = count_ref[0, 0, v]
        for by in range(downs):
            for t in range(tiles):
                pair = []
                for side in range(2):
                    r = by * (width // BS) + 2 * t + side
                    spot = owner_ref[0, 0, v * blocks + r] * patches + slot_ref[0, 0, v * blocks + r]
                    pair.append(jnp.where(r < limit, spot, patch_total))
                for m in range(2):
                    even = image[m, t, pl.ds(by * BS, BS // 2, stride=2), :]
                    odd = image[m, t, pl.ds(by * BS + 1, BS // 2, stride=2), :]
                    left = jnp.where(low_lanes, even, pltpu.roll(odd, BS, 1))
                    right = jnp.where(low_lanes, pltpu.roll(even, BS, 1), odd)
                    total[pair[0], m] += left
                    total[pair[1], m] += right
    pay_ref[...] = total[0:patch_total].astype(BF16)


def merge_kernel(
    n, skies, patches, pay_ref, sum_ref, weight_ref, out_ref, landed, merged, edge, halo, send, recv, edge_send, edge_recv
):
    sky = lax.axis_index("sky")
    me = lax.axis_index("tile")
    peers = [lax.rem(me + k, n) for k in range(1, n)]
    barrier = greet([(sky, peer) for peer in peers])
    has_low = sky > 0
    has_high = sky < skies - 1

    @pl.when(has_low)
    def _():
        pl.semaphore_signal(barrier, inc=1, device_id=(sky - 1, me), device_id_type=MESH)

    @pl.when(has_high)
    def _():
        pl.semaphore_signal(barrier, inc=1, device_id=(sky + 1, me), device_id_type=MESH)

    around = jnp.where(has_low, 1, 0) + jnp.where(has_high, 1, 0)
    pl.semaphore_wait(barrier, n - 1 + around)
    copies = []
    for k, peer in enumerate(peers):
        copy = pltpu.make_async_remote_copy(
            src_ref=pay_ref.at[pl.ds(peer * patches, patches)],
            dst_ref=landed.at[k],
            send_sem=send.at[k],
            recv_sem=recv.at[k],
            device_id=(sky, peer),
            device_id_type=MESH,
        )
        copy.start()
        copies.append(copy)
    summed = pay_ref[pl.ds(me * patches, patches)].astype(F32)
    for k, copy in enumerate(copies):
        copy.wait_recv()
        summed = summed + landed[k].astype(F32)
    merged[...] = summed
    edge[0] = summed[0].astype(BF16)
    edge[1] = summed[patches - 1].astype(BF16)
    to_low = pltpu.make_async_remote_copy(
        src_ref=edge.at[0],
        dst_ref=halo.at[1],
        send_sem=edge_send.at[0],
        recv_sem=edge_recv.at[1],
        device_id=(sky - 1, me),
        device_id_type=MESH,
    )
    to_high = pltpu.make_async_remote_copy(
        src_ref=edge.at[1],
        dst_ref=halo.at[0],
        send_sem=edge_send.at[1],
        recv_sem=edge_recv.at[0],
        device_id=(sky + 1, me),
        device_id_type=MESH,
    )

    @pl.when(has_low)
    def _():
        to_low.start()

    @pl.when(has_high)
    def _():
        to_high.start()

    for copy in copies:
        copy.wait_send()

    @pl.when(has_low)
    def _():
        to_low.wait_send()
        to_high.wait_recv()
        merged[0] += halo[0].astype(F32)

    @pl.when(has_high)
    def _():
        to_high.wait_send()
        to_low.wait_recv()
        merged[patches - 1] += halo[1].astype(F32)

    for row in range(BS * BS // LANES):
        span = slice(row * LANES, (row + 1) * LANES)
        out_ref[0, 0, :, span] = (sum_ref[0, 0, :, span] + merged[:, 0, row, :]) / (
            weight_ref[0, 0, :, span] + merged[:, 1, row, :]
        )


def shards(
    science,
    inverse_variance,
    template,
    filters,
    kernel_index,
    spatial_coeff,
    visit_offset,
    block_count,
    block_owner,
    block_slot,
    coadd_sum,
    coadd_weight,
    *,
    n,
    skies,
):
    visits, height, width = science.shape[2:]
    basis = filters.shape[0]
    patches = coadd_sum.shape[2]
    tiles = width // LANES
    strip = height * tiles // n
    patch_total = n * patches
    rows = BS * BS // LANES
    vmem = pl.BlockSpec(memory_space=pltpu.VMEM)
    smem = pl.BlockSpec(memory_space=pltpu.SMEM)
    dma = pltpu.SemaphoreType.DMA
    limit = 40 * 1024 * 1024
    strips = pl.pallas_call(
        functools.partial(align_kernel, n, visits),
        out_shape=jax.ShapeDtypeStruct((n, visits, strip, LANES), BF16),
        in_specs=[smem, vmem],
        out_specs=vmem,
        scratch_shapes=[
            pltpu.VMEM((n * strip, LANES), BF16),
            pltpu.VMEM((n, strip, LANES), BF16),
            pltpu.VMEM((n - 1, visits, strip, LANES), BF16),
            dma((n - 1,)),
            dma((n - 1,)),
            dma((n - 1,)),
            dma((n - 1,)),
        ],
        compiler_params=pltpu.CompilerParams(
            collective_id=0, has_side_effects=True, vmem_limit_bytes=limit
        ),
        name="align",
    )(visit_offset, template)
    difference, pay = pl.pallas_call(
        functools.partial(match_kernel, patch_total, patches),
        out_shape=(
            jax.ShapeDtypeStruct(science.shape, F32),
            jax.ShapeDtypeStruct((patch_total, 2, rows, LANES), BF16),
        ),
        in_specs=[vmem] * 6 + [smem] * 3,
        out_specs=(vmem, vmem),
        scratch_shapes=[
            pltpu.VMEM((visits, basis * height, width), BF16),
            pltpu.VMEM((3 * LANES, basis * LANES), BF16),
            pltpu.VMEM((visits, 2 * height, basis * LANES), BF16),
            pltpu.VMEM((visits, 2 * height, basis * LANES), BF16),
            pltpu.VMEM((2, tiles, height, LANES), F32),
            pltpu.VMEM((patch_total + 1, 2, rows, LANES), F32),
        ],
        compiler_params=pltpu.CompilerParams(vmem_limit_bytes=limit),
        name="match",
    )(
        strips,
        filters,
        kernel_index,
        spatial_coeff,
        science,
        inverse_variance,
        block_count,
        block_owner,
        block_slot,
    )
    coadd = pl.pallas_call(
        functools.partial(merge_kernel, n, skies, patches),
        out_shape=jax.ShapeDtypeStruct(coadd_sum.shape, F32),
        in_specs=[vmem] * 3,
        out_specs=vmem,
        scratch_shapes=[
            pltpu.VMEM((n - 1, patches, 2, rows, LANES), BF16),
            pltpu.VMEM((patches, 2, rows, LANES), F32),
            pltpu.VMEM((2, 2, rows, LANES), BF16),
            pltpu.VMEM((2, 2, rows, LANES), BF16),
            dma((n - 1,)),
            dma((n - 1,)),
            dma((2,)),
            dma((2,)),
        ],
        compiler_params=pltpu.CompilerParams(
            collective_id=1, has_side_effects=True, vmem_limit_bytes=limit
        ),
        name="merge",
    )(pay, coadd_sum, coadd_weight)
    return difference, coadd


def solution(mesh):
    return jax.shard_map(
        functools.partial(shards, n=mesh.shape["tile"], skies=mesh.shape["sky"]),
        mesh=mesh,
        in_specs=(
            P("sky", "tile", None, None, None),
            P("sky", "tile", None, None, None),
            P("sky", "tile", None, None),
            P(),
            P(),
            P("sky", "tile", None, None, None),
            P("sky", None),
            P("sky", "tile", None),
            P("sky", "tile", None),
            P("sky", "tile", None),
            P("sky", "tile", None, None),
            P("sky", "tile", None, None),
        ),
        out_specs=(P("sky", "tile", None, None, None), P("sky", "tile", None, None)),
        check_vma=False,
    )
```

time: 176 us -> 34.4 us (0.20)
  waiting for transfers between devices: 60.3 us -> 0 us
  matrix products: 48.5 us -> 0 us
  Pallas kernels: 0 us -> 27.9 us
  local copies, waits for them, and re-layouts: 21.7 us -> 5.51 us
  between operations: 16.6 us -> 0.71 us
  starting transfers between devices: 14.1 us -> 0 us
  other arithmetic: 13.9 us -> 0 us
    unnamed x2 -> x0, waiting for transfers between devices: 52.8 us -> none
    dot_general x5 -> x0, matrix products: 48.5 us -> none  [the longest x1 36.5 us: shards(): jnp.einsum('kyg,vkgw->vyw', band_stack, operand_stack, precision=lax.Prec...]
    pallas_call x0 -> x3, Pallas kernels: none -> 27.9 us  [the longest x1 12.4 us: shards(): pl.pallas_call(functools.partial(align_kernel, n, visits), out_shape=jax....]
    all_to_all x2 -> x0, starting transfers between devices: 9.38 us -> none  [the longest x1 5.18 us: shards(): lax.all_to_all(strips, 'tile', split_axis=0, concat_axis=0, tiled=True)]
    reshape x10 -> x0, local copies, waits for them, and re-layouts: 8.8 us -> none  [the longest x2 5.65 us: shards(): filtered.astype(jnp.bfloat16)]
    mul x1 -> x0, other arithmetic: 6.19 us -> none  [shards(): downward[None, :, None] * column_band]
    slice x7 -> x0, local copies, waits for them, and re-layouts: 5.14 us -> none  [the longest x2 1.82 us: shards(): taps_all[None, :, q, None]]
    ppermute x2 -> x0, starting transfers between devices: 4.53 us -> none  [the longest x1 3.24 us: with_halo(): lax.ppermute(tail, axis, [(i, (i + 1) % count) for i in range(ends)])]
  transfers between devices with their start and end apart: 5 -> 0, of which waited for: 3 -> 0; matrix products, arithmetic and copies ran while one was open for 15% -> 0% of each run, Pallas kernels for 0% -> 0%
where the time goes in v1:
time: 34.4 us; the launch traced here: 34.1 us
  Pallas kernels  27.9 us (81%)
  local copies, waits for them, and re-layouts  5.51 us (16%)
  between operations  0.71 us (2%)
    pallas_call x1, Pallas kernels, shards(): pl.pallas_call(functools.partial(align_kernel, n, visits), out_shape=jax....  12.4 us
    pallas_call x1, Pallas kernels, shards(): pl.pallas_call(functools.partial(merge_kernel, n, skies, patches), out_sh...  11.2 us
    unnamed x29, local copies, waits for them, and re-layouts  5.51 us
    pallas_call x1, Pallas kernels, shards(): pl.pallas_call(functools.partial(match_kernel, patch_total, patches), out...  4.28 us

profile of v1, /device:TPU:0, one launch (start us, length us, event | category | flops | bytes accessed | tf_op | source)
XLA Modules:
  0.0 34.1 jit_solution(11471752489823277254)
XLA Ops:
  0.6 0.0 copy-start.1
  0.6 0.0 copy-start.2
  0.7 0.9 %copy-done.2 = bf16[1,1,128,512]{3,2,1,0:T(8,128)(2,1)S(1)} copy-done((bf16[1,1,128,512]{3,2,1,0:T(8,128)(2,1)S(1)}, bf16[1,1,128,512]{3,2,1,0:T(8,128)(2,1)}, u32[]{:S(2)}) %copy-start.2) | copy-done | bytes 131096
  1.6 0.0 copy-start.4
  1.6 0.7 %copy-done.4 = s32[1,2]{1,0:T(1,128)S(1)} copy-done((s32[1,2]{1,0:T(1,128)S(1)}, s32[1,2]{1,0:T(1,128)}, u32[]{:S(2)}) %copy-start.4) | copy-done | bytes 32
  2.2 0.0 copy-start.11
  2.2 12.4 %align.1.strips_ref = bf16[8,2,64,128]{3,2,1,0:T(8,128)(2,1)S(1)} custom-call(s32[1,2]{1,0:T(1,128)S(1)} %copy-done.4, bf16[1,1,128,512]{3,2,1,0:T(8,128)(2,1)S(1)} %copy-done.2), custom_call_target="tpu_custom_call" | custom-call | tf_op jit(solution)/shard_map/align/pallas_call | solution.py:320
  14.7 0.0 copy-done.11
  14.7 0.0 copy-start.10
  14.7 0.1 copy.14.index_ref
  14.8 0.6 %copy-done.10 = f32[1,1,2,3,20]{4,2,3,1,0:T(2,128)S(1)} copy-done((f32[1,1,2,3,20]{4,2,3,1,0:T(2,128)S(1)}, f32[1,1,2,3,20]{4,2,3,1,0:T(2,128)}, u32[]{:S(2)}) %copy-start.10) | copy-done | bytes 504
  15.4 0.0 copy-start.3
  15.4 0.0 copy-start.5
  15.4 0.0 copy-start.6
  15.4 0.0 copy-start.7
  15.4 0.0 copy-done.1
  15.4 0.7 %copy-done.3 = bf16[8,21]{1,0:T(8,128)(2,1)S(1)} copy-done((bf16[8,21]{1,0:T(8,128)(2,1)S(1)}, bf16[8,21]{1,0:T(8,128)(2,1)}, u32[]{:S(2)}) %copy-start.3) | copy-done | bytes 360
  16.0 0.0 copy-done.5
  16.0 0.0 copy-done.6
  16.0 0.0 copy-done.7
  16.1 0.0 copy-start
  16.1 1.0 %copy-done = f32[1,1,2,128,512]{4,3,2,1,0:T(8,128)S(1)} copy-done((f32[1,1,2,128,512]{4,3,2,1,0:T(8,128)S(1)}, f32[1,1,2,128,512]{4,3,2,1,0:T(8,128)}, u32[]{:S(2)}) %copy-start) | copy-done | bytes 524312
  17.1 0.0 copy-start.8
  17.1 4.3 %match.1 = (f32[1,1,2,128,512]{4,3,2,1,0:T(8,128)}, bf16[24,2,32,128]{3,2,1,0:T(8,128)(2,1)S(1)}) custom-call(bf16[8,2,64,128]{3,2,1,0:T(8,128)(2,1)S(1)} %align.1.strips_ref, bf16[8,21]{1,0:T(8,128)(2,1)S(1)} %copy-done.3, s32[20,2]{1,0:T(8,128)S(1)} %copy.14.index_ref, f32[1,1,2,3,20]{4,3,2,1,0:T(4,128)S(1)} %copy.15.coeff_ref, ...), custom_call_target="tpu_custom_call" | custom-call | tf_op jit(solution)/shard_map/match/pallas_call | solution.py:339
  21.4 0.0 copy-done.8
  21.4 0.0 copy-start.9
  21.4 0.8 %copy-done.9 = f32[1,1,3,4096]{3,1,2,0:T(1,128)S(1)} copy-done((f32[1,1,3,4096]{3,1,2,0:T(1,128)S(1)}, f32[1,1,3,4096]{3,1,2,0:T(1,128)}, u32[]{:S(2)}) %copy-start.9) | copy-done | bytes 49176
  22.2 11.2 %merge.1 = f32[1,1,3,4096]{3,2,1,0:T(4,128)S(1)} custom-call(bf16[24,2,32,128]{3,2,1,0:T(8,128)(2,1)S(1)} %get-tuple-element.5.pay_ref, f32[1,1,3,4096]{3,2,1,0:T(4,128)S(1)} %copy.16.sum_ref, f32[1,1,3,4096]{3,2,1,0:T(4,128)S(1)} %copy.17.weight_ref), custom_call_target="tpu_custom_call" | custom-call | tf_op jit(solution)/shard_map/merge/pallas_call | solution.py:368
  33.5 0.7 %copy.18 = f32[1,1,3,4096]{3,1,2,0:T(1,128)} copy(f32[1,1,3,4096]{3,2,1,0:T(4,128)S(1)} %merge.1) | data formatting | bytes 98304
  (3 shorter events, 0.1 us)
Async XLA Ops:
  0.6 14.8 %copy-start.1 = (bf16[1,1,2,128,512]{4,3,2,1,0:T(8,128)(2,1)S(1)}, bf16[1,1,2,128,512]{4,3,2,1,0:T(8,128)(2,1)}, u32[]{:S(2)}) copy-start(bf16[1,1,2,128,512]{4,3,2,1,0:T(8,128)(2,1)} %inverse_ref.1) | copy-start | bytes 786436
  0.6 0.9 %copy-start.2 = (bf16[1,1,128,512]{3,2,1,0:T(8,128)(2,1)S(1)}, bf16[1,1,128,512]{3,2,1,0:T(8,128)(2,1)}, u32[]{:S(2)}) copy-start(bf16[1,1,128,512]{3,2,1,0:T(8,128)(2,1)} %template_ref.1) | copy-start | bytes 393220
  1.6 0.7 %copy-start.4 = (s32[1,2]{1,0:T(1,128)S(1)}, s32[1,2]{1,0:T(1,128)}, u32[]{:S(2)}) copy-start(s32[1,2]{1,0:T(1,128)} %offset_ref.1) | copy-start | bytes 28
  2.2 12.4 %copy-start.11 = (s32[20,2]{0,1:T(2,128)S(1)}, s32[20,2]{0,1:T(2,128)}, u32[]{:S(2)}) copy-start(s32[20,2]{0,1:T(2,128)} %param.16) | copy-start | bytes 484
  14.7 0.7 %copy-start.10 = (f32[1,1,2,3,20]{4,2,3,1,0:T(2,128)S(1)}, f32[1,1,2,3,20]{4,2,3,1,0:T(2,128)}, u32[]{:S(2)}) copy-start(f32[1,1,2,3,20]{4,2,3,1,0:T(2,128)} %param.17) | copy-start | bytes 1444
  15.4 0.7 %copy-start.3 = (bf16[8,21]{1,0:T(8,128)(2,1)S(1)}, bf16[8,21]{1,0:T(8,128)(2,1)}, u32[]{:S(2)}) copy-start(bf16[8,21]{1,0:T(8,128)(2,1)} %filters_ref.1) | copy-start | bytes 1012
  15.4 0.7 %copy-start.5 = (s32[1,1,2]{2,1,0:T(1,128)S(1)}, s32[1,1,2]{2,1,0:T(1,128)}, u32[]{:S(2)}) copy-start(s32[1,1,2]{2,1,0:T(1,128)} %count_ref.1) | copy-start | bytes 28
  15.4 0.7 %copy-start.6 = (s32[1,1,32]{2,1,0:T(1,128)S(1)}, s32[1,1,32]{2,1,0:T(1,128)}, u32[]{:S(2)}) copy-start(s32[1,1,32]{2,1,0:T(1,128)} %owner_ref.1) | copy-start | bytes 388
  15.4 0.7 %copy-start.7 = (s32[1,1,32]{2,1,0:T(1,128)S(1)}, s32[1,1,32]{2,1,0:T(1,128)}, u32[]{:S(2)}) copy-start(s32[1,1,32]{2,1,0:T(1,128)} %slot_ref.1) | copy-start | bytes 388
  16.1 1.0 %copy-start = (f32[1,1,2,128,512]{4,3,2,1,0:T(8,128)S(1)}, f32[1,1,2,128,512]{4,3,2,1,0:T(8,128)}, u32[]{:S(2)}) copy-start(f32[1,1,2,128,512]{4,3,2,1,0:T(8,128)} %science_ref.1) | copy-start | bytes 1572868
  17.1 4.3 %copy-start.8 = (f32[1,1,3,4096]{3,1,2,0:T(1,128)S(1)}, f32[1,1,3,4096]{3,1,2,0:T(1,128)}, u32[]{:S(2)}) copy-start(f32[1,1,3,4096]{3,1,2,0:T(1,128)} %param.22) | copy-start | bytes 147460
  21.4 0.8 %copy-start.9 = (f32[1,1,3,4096]{3,1,2,0:T(1,128)S(1)}, f32[1,1,3,4096]{3,1,2,0:T(1,128)}, u32[]{:S(2)}) copy-start(f32[1,1,3,4096]{3,1,2,0:T(1,128)} %param.23) | copy-start | bytes 147460

commit v2 on v1

--- a/solution.py
+++ b/solution.py
@@ -84,8 +84,8 @@
     filters_ref,
     index_ref,
     coeff_ref,
-    science_ref,
-    inverse_ref,
+    science_hbm,
+    inverse_hbm,
     count_ref,
     owner_ref,
     slot_ref,
@@ -97,7 +97,16 @@
     band_low,
     image,
     total,
+    science_ref,
+    inverse_ref,
+    arrived,
 ):
+    fetches = [
+        pltpu.make_async_copy(science_hbm, science_ref, arrived.at[0]),
+        pltpu.make_async_copy(inverse_hbm, inverse_ref, arrived.at[1]),
+    ]
+    for fetch in fetches:
+        fetch.start()
     n, visits, strip, lanes = strips_ref.shape
     height, width = science_ref.shape[-2:]
     tiles = width // LANES
@@ -168,6 +177,8 @@
                 ]
 
     total[...] = jnp.zeros_like(total)
+    for fetch in fetches:
+        fetch.wait()
     x_id = lax.broadcasted_iota(jnp.int32, (1, width), 1).astype(F32)
     rightward = (2.0 * x_id + (1.0 - width)) / width
     low_lanes = lax.broadcasted_iota(jnp.int32, (BS // 2, LANES), 1) < BS
@@ -342,7 +353,7 @@
             jax.ShapeDtypeStruct(science.shape, F32),
             jax.ShapeDtypeStruct((patch_total, 2, rows, LANES), BF16),
         ),
-        in_specs=[vmem] * 6 + [smem] * 3,
+        in_specs=[vmem] * 4 + [pl.BlockSpec(memory_space=pl.ANY)] * 2 + [smem] * 3,
         out_specs=(vmem, vmem),
         scratch_shapes=[
             pltpu.VMEM((visits, basis * height, width), BF16),
@@ -351,6 +362,9 @@
             pltpu.VMEM((visits, 2 * height, basis * LANES), BF16),
             pltpu.VMEM((2, tiles, height, LANES), F32),
             pltpu.VMEM((patch_total + 1, 2, rows, LANES), F32),
+            pltpu.VMEM(science.shape, F32),
+            pltpu.VMEM(inverse_variance.shape, BF16),
+            dma((2,)),
         ],
         compiler_params=pltpu.CompilerParams(vmem_limit_bytes=limit),
         name="match",

time: 34.4 us -> 34.7 us (level)
  no operation moved by 1% of the time
where the time goes in v2:
time: 34.7 us; the launch traced here: 34.4 us
  Pallas kernels  28.2 us (81%)
  local copies, waits for them, and re-layouts  5.5 us (16%)
  between operations  0.74 us (2%)
    pallas_call x1, Pallas kernels, shards(): pl.pallas_call(functools.partial(align_kernel, n, visits), out_shape=jax....  12.4 us
    pallas_call x1, Pallas kernels, shards(): pl.pallas_call(functools.partial(merge_kernel, n, skies, patches), out_sh...  11.2 us
    unnamed x29, local copies, waits for them, and re-layouts  5.5 us
    pallas_call x1, Pallas kernels, shards(): pl.pallas_call(functools.partial(match_kernel, patch_total, patches), out...  4.56 us

profile of v2, /device:TPU:0, one launch (start us, length us, event | category | flops | bytes accessed | tf_op | source)
XLA Modules:
  0.0 34.4 jit_solution(9985821266163883861)
XLA Ops:
  0.6 0.0 copy-start.1
  0.6 0.0 copy-start.2
  0.7 0.9 %copy-done.2 = bf16[1,1,128,512]{3,2,1,0:T(8,128)(2,1)S(1)} copy-done((bf16[1,1,128,512]{3,2,1,0:T(8,128)(2,1)S(1)}, bf16[1,1,128,512]{3,2,1,0:T(8,128)(2,1)}, u32[]{:S(2)}) %copy-start.2) | copy-done | bytes 131096
  1.6 0.0 copy-start.4
  1.6 0.7 %copy-done.4 = s32[1,2]{1,0:T(1,128)S(1)} copy-done((s32[1,2]{1,0:T(1,128)S(1)}, s32[1,2]{1,0:T(1,128)}, u32[]{:S(2)}) %copy-start.4) | copy-done | bytes 32
  2.2 0.0 copy-start.11
  2.2 12.4 %align.1.strips_ref = bf16[8,2,64,128]{3,2,1,0:T(8,128)(2,1)S(1)} custom-call(s32[1,2]{1,0:T(1,128)S(1)} %copy-done.4, bf16[1,1,128,512]{3,2,1,0:T(8,128)(2,1)S(1)} %copy-done.2), custom_call_target="tpu_custom_call" | custom-call | tf_op jit(solution)/shard_map/align/pallas_call | solution.py:331
  14.7 0.0 copy-done.11
  14.7 0.0 copy-start.10
  14.7 0.1 copy.14.index_ref
  14.8 0.6 %copy-done.10 = f32[1,1,2,3,20]{4,2,3,1,0:T(2,128)S(1)} copy-done((f32[1,1,2,3,20]{4,2,3,1,0:T(2,128)S(1)}, f32[1,1,2,3,20]{4,2,3,1,0:T(2,128)}, u32[]{:S(2)}) %copy-start.10) | copy-done | bytes 504
  15.4 0.0 copy-start.3
  15.4 0.0 copy-start.5
  15.4 0.0 copy-start.6
  15.4 0.0 copy-start.7
  15.4 0.0 copy-done.1
  15.4 0.7 %copy-done.3 = bf16[8,21]{1,0:T(8,128)(2,1)S(1)} copy-done((bf16[8,21]{1,0:T(8,128)(2,1)S(1)}, bf16[8,21]{1,0:T(8,128)(2,1)}, u32[]{:S(2)}) %copy-start.3) | copy-done | bytes 360
  16.0 0.0 copy-done.5
  16.0 0.0 copy-done.6
  16.0 0.0 copy-done.7
  16.1 0.0 copy-start
  16.1 1.0 %copy-done = f32[1,1,2,128,512]{4,3,2,1,0:T(8,128)S(1)} copy-done((f32[1,1,2,128,512]{4,3,2,1,0:T(8,128)S(1)}, f32[1,1,2,128,512]{4,3,2,1,0:T(8,128)}, u32[]{:S(2)}) %copy-start) | copy-done | bytes 524312
  17.1 0.0 copy-start.8
  17.1 4.6 %match.1 = (f32[1,1,2,128,512]{4,3,2,1,0:T(8,128)}, bf16[24,2,32,128]{3,2,1,0:T(8,128)(2,1)S(1)}) custom-call(bf16[8,2,64,128]{3,2,1,0:T(8,128)(2,1)S(1)} %align.1.strips_ref, bf16[8,21]{1,0:T(8,128)(2,1)S(1)} %copy-done.3, s32[20,2]{1,0:T(8,128)S(1)} %copy.14.index_ref, f32[1,1,2,3,20]{4,3,2,1,0:T(4,128)S(1)} %copy.15.coeff_ref, ...), custom_call_target="tpu_custom_call" | custom-call | tf_op jit(solution)/shard_map/match/pallas_call | solution.py:350
  21.7 0.0 copy-done.8
  21.7 0.0 copy-start.9
  21.7 0.7 %copy-done.9 = f32[1,1,3,4096]{3,1,2,0:T(1,128)S(1)} copy-done((f32[1,1,3,4096]{3,1,2,0:T(1,128)S(1)}, f32[1,1,3,4096]{3,1,2,0:T(1,128)}, u32[]{:S(2)}) %copy-start.9) | copy-done | bytes 49176
  22.5 11.2 %merge.1 = f32[1,1,3,4096]{3,2,1,0:T(4,128)S(1)} custom-call(bf16[24,2,32,128]{3,2,1,0:T(8,128)(2,1)S(1)} %get-tuple-element.5.pay_ref, f32[1,1,3,4096]{3,2,1,0:T(4,128)S(1)} %copy.16.sum_ref, f32[1,1,3,4096]{3,2,1,0:T(4,128)S(1)} %copy.17.weight_ref), custom_call_target="tpu_custom_call" | custom-call | tf_op jit(solution)/shard_map/merge/pallas_call | solution.py:382
  33.8 0.7 %copy.18 = f32[1,1,3,4096]{3,1,2,0:T(1,128)} copy(f32[1,1,3,4096]{3,2,1,0:T(4,128)S(1)} %merge.1) | data formatting | bytes 98304
  (3 shorter events, 0.1 us)
Async XLA Ops:
  0.6 14.8 %copy-start.1 = (bf16[1,1,2,128,512]{4,3,2,1,0:T(8,128)(2,1)S(1)}, bf16[1,1,2,128,512]{4,3,2,1,0:T(8,128)(2,1)}, u32[]{:S(2)}) copy-start(bf16[1,1,2,128,512]{4,3,2,1,0:T(8,128)(2,1)} %inverse_hbm.1) | copy-start | bytes 786436
  0.6 0.9 %copy-start.2 = (bf16[1,1,128,512]{3,2,1,0:T(8,128)(2,1)S(1)}, bf16[1,1,128,512]{3,2,1,0:T(8,128)(2,1)}, u32[]{:S(2)}) copy-start(bf16[1,1,128,512]{3,2,1,0:T(8,128)(2,1)} %template_ref.1) | copy-start | bytes 393220
  1.6 0.7 %copy-start.4 = (s32[1,2]{1,0:T(1,128)S(1)}, s32[1,2]{1,0:T(1,128)}, u32[]{:S(2)}) copy-start(s32[1,2]{1,0:T(1,128)} %offset_ref.1) | copy-start | bytes 28
  2.2 12.4 %copy-start.11 = (s32[20,2]{0,1:T(2,128)S(1)}, s32[20,2]{0,1:T(2,128)}, u32[]{:S(2)}) copy-start(s32[20,2]{0,1:T(2,128)} %param.16) | copy-start | bytes 484
  14.7 0.7 %copy-start.10 = (f32[1,1,2,3,20]{4,2,3,1,0:T(2,128)S(1)}, f32[1,1,2,3,20]{4,2,3,1,0:T(2,128)}, u32[]{:S(2)}) copy-start(f32[1,1,2,3,20]{4,2,3,1,0:T(2,128)} %param.17) | copy-start | bytes 1444
  15.4 0.7 %copy-start.3 = (bf16[8,21]{1,0:T(8,128)(2,1)S(1)}, bf16[8,21]{1,0:T(8,128)(2,1)}, u32[]{:S(2)}) copy-start(bf16[8,21]{1,0:T(8,128)(2,1)} %filters_ref.1) | copy-start | bytes 1012
  15.4 0.7 %copy-start.5 = (s32[1,1,2]{2,1,0:T(1,128)S(1)}, s32[1,1,2]{2,1,0:T(1,128)}, u32[]{:S(2)}) copy-start(s32[1,1,2]{2,1,0:T(1,128)} %count_ref.1) | copy-start | bytes 28
  15.4 0.7 %copy-start.6 = (s32[1,1,32]{2,1,0:T(1,128)S(1)}, s32[1,1,32]{2,1,0:T(1,128)}, u32[]{:S(2)}) copy-start(s32[1,1,32]{2,1,0:T(1,128)} %owner_ref.1) | copy-start | bytes 388
  15.4 0.7 %copy-start.7 = (s32[1,1,32]{2,1,0:T(1,128)S(1)}, s32[1,1,32]{2,1,0:T(1,128)}, u32[]{:S(2)}) copy-start(s32[1,1,32]{2,1,0:T(1,128)} %slot_ref.1) | copy-start | bytes 388
  16.1 1.0 %copy-start = (f32[1,1,2,128,512]{4,3,2,1,0:T(8,128)S(1)}, f32[1,1,2,128,512]{4,3,2,1,0:T(8,128)}, u32[]{:S(2)}) copy-start(f32[1,1,2,128,512]{4,3,2,1,0:T(8,128)} %science_hbm.1) | copy-start | bytes 1572868
  17.1 4.6 %copy-start.8 = (f32[1,1,3,4096]{3,1,2,0:T(1,128)S(1)}, f32[1,1,3,4096]{3,1,2,0:T(1,128)}, u32[]{:S(2)}) copy-start(f32[1,1,3,4096]{3,1,2,0:T(1,128)} %param.22) | copy-start | bytes 147460
  21.7 0.8 %copy-start.9 = (f32[1,1,3,4096]{3,1,2,0:T(1,128)S(1)}, f32[1,1,3,4096]{3,1,2,0:T(1,128)}, u32[]{:S(2)}) copy-start(f32[1,1,3,4096]{3,1,2,0:T(1,128)} %param.23) | copy-start | bytes 147460

commit v3 on v2

--- a/solution.py
+++ b/solution.py
@@ -327,7 +327,6 @@
     vmem = pl.BlockSpec(memory_space=pltpu.VMEM)
     smem = pl.BlockSpec(memory_space=pltpu.SMEM)
     dma = pltpu.SemaphoreType.DMA
-    limit = 40 * 1024 * 1024
     strips = pl.pallas_call(
         functools.partial(align_kernel, n, visits),
         out_shape=jax.ShapeDtypeStruct((n, visits, strip, LANES), BF16),
@@ -343,7 +342,7 @@
             dma((n - 1,)),
         ],
         compiler_params=pltpu.CompilerParams(
-            collective_id=0, has_side_effects=True, vmem_limit_bytes=limit
+            collective_id=0, has_side_effects=True
         ),
         name="align",
     )(visit_offset, template)
@@ -366,7 +365,7 @@
             pltpu.VMEM(inverse_variance.shape, BF16),
             dma((2,)),
         ],
-        compiler_params=pltpu.CompilerParams(vmem_limit_bytes=limit),
+        compiler_params=pltpu.CompilerParams(),
         name="match",
     )(
         strips,
@@ -395,7 +394,7 @@
             dma((2,)),
         ],
         compiler_params=pltpu.CompilerParams(
-            collective_id=1, has_side_effects=True, vmem_limit_bytes=limit
+            collective_id=1, has_side_effects=True
         ),
         name="merge",
     )(pay, coadd_sum, coadd_weight)

time: 34.7 us -> 36.7 us (1.058)
  Pallas kernels: 28.2 us -> 31.4 us
  local copies, waits for them, and re-layouts: 5.5 us -> 4.28 us
    pallas_call x1, Pallas kernels: 11.2 us -> 12.9 us  [shards(): pl.pallas_call(functools.partial(merge_kernel, n, skies, patches), out_sh...]
    unnamed x29 -> x13, local copies, waits for them, and re-layouts: 5.5 us -> 4.28 us
    pallas_call x1, Pallas kernels: 12.4 us -> 13.5 us  [shards(): pl.pallas_call(functools.partial(align_kernel, n, visits), out_shape=jax....]
    pallas_call x1, Pallas kernels: 4.56 us -> 5.05 us  [shards(): pl.pallas_call(functools.partial(match_kernel, patch_total, patches), out...]
where the time goes in v3:
time: 36.7 us; the launch traced here: 36.4 us
  Pallas kernels  31.4 us (86%)
  local copies, waits for them, and re-layouts  4.28 us (12%)
  between operations  0.7 us (2%)
    pallas_call x1, Pallas kernels, shards(): pl.pallas_call(functools.partial(align_kernel, n, visits), out_shape=jax....  13.5 us
    pallas_call x1, Pallas kernels, shards(): pl.pallas_call(functools.partial(merge_kernel, n, skies, patches), out_sh...  12.9 us
    pallas_call x1, Pallas kernels, shards(): pl.pallas_call(functools.partial(match_kernel, patch_total, patches), out...  5.05 us
    unnamed x13, local copies, waits for them, and re-layouts  4.28 us

profile of v3, /device:TPU:0, one launch (start us, length us, event | category | flops | bytes accessed | tf_op | source)
XLA Modules:
  0.0 36.4 jit_solution(3152321310562383515)
XLA Ops:
  0.6 0.0 copy-start.3
  0.6 13.5 %align.1.strips_ref = bf16[8,2,64,128]{3,2,1,0:T(8,128)(2,1)} custom-call(s32[1,2]{1,0:T(1,128)} %offset_ref.1, bf16[1,1,128,512]{3,2,1,0:T(8,128)(2,1)} %template_ref.1), custom_call_target="tpu_custom_call" | custom-call | tf_op jit(solution)/shard_map/align/pallas_call | solution.py:330
  14.1 0.0 copy-done.3
  14.2 0.0 copy-start.2
  14.2 0.7 %copy.14.index_ref = s32[20,2]{1,0:T(8,128)} copy(s32[20,2]{0,1:T(2,128)S(1)} %copy-done.3) | data formatting | bytes 320 | tf_op args[4]
  14.9 0.0 copy-done.2
  14.9 0.6 %copy.15.coeff_ref = f32[1,1,2,3,20]{4,3,2,1,0:T(4,128)} copy(f32[1,1,2,3,20]{4,2,3,1,0:T(2,128)S(1)} %copy-done.2) | data formatting | bytes 960 | tf_op args[5]
  15.5 0.0 copy-start
  15.5 5.1 %match.1 = (f32[1,1,2,128,512]{4,3,2,1,0:T(8,128)}, bf16[24,2,32,128]{3,2,1,0:T(8,128)(2,1)}) custom-call(bf16[8,2,64,128]{3,2,1,0:T(8,128)(2,1)} %align.1.strips_ref, bf16[8,21]{1,0:T(8,128)(2,1)} %filters_ref.1, s32[20,2]{1,0:T(8,128)} %copy.14.index_ref, f32[1,1,2,3,20]{4,3,2,1,0:T(4,128)} %copy.15.coeff_ref, f32[1,1,2,128,512]{4,3,2,1,0:T(8,128)} %science_hbm.1, ...), custom_call_target="tpu_custom_call" | custom-call | tf_op jit(solution)/shard_map/match/pallas_call | solution.py:349
  20.5 0.0 copy-done
  20.5 0.0 copy-start.1
  20.5 0.7 %copy.16.sum_ref = f32[1,1,3,4096]{3,2,1,0:T(4,128)} copy(f32[1,1,3,4096]{3,1,2,0:T(1,128)S(1)} %copy-done) | data formatting | bytes 98304 | tf_op args[10]
  21.2 0.1 copy-done.1
  21.3 0.7 %copy.17.weight_ref = f32[1,1,3,4096]{3,2,1,0:T(4,128)} copy(f32[1,1,3,4096]{3,1,2,0:T(1,128)S(1)} %copy-done.1) | data formatting | bytes 98304 | tf_op args[11]
  22.0 12.9 %merge.1 = f32[1,1,3,4096]{3,2,1,0:T(4,128)} custom-call(bf16[24,2,32,128]{3,2,1,0:T(8,128)(2,1)} %get-tuple-element.5.pay_ref, f32[1,1,3,4096]{3,2,1,0:T(4,128)} %copy.16.sum_ref, f32[1,1,3,4096]{3,2,1,0:T(4,128)} %copy.17.weight_ref), custom_call_target="tpu_custom_call" | custom-call | tf_op jit(solution)/shard_map/merge/pallas_call | solution.py:381
  34.9 1.5 %copy.18 = f32[1,1,3,4096]{3,1,2,0:T(1,128)} copy(f32[1,1,3,4096]{3,2,1,0:T(4,128)} %merge.1) | data formatting | bytes 98304
Async XLA Ops:
  0.6 13.5 %copy-start.3 = (s32[20,2]{0,1:T(2,128)S(1)}, s32[20,2]{0,1:T(2,128)}, u32[]{:S(2)}) copy-start(s32[20,2]{0,1:T(2,128)} %param.16) | copy-start | bytes 484
  14.2 0.7 %copy-start.2 = (f32[1,1,2,3,20]{4,2,3,1,0:T(2,128)S(1)}, f32[1,1,2,3,20]{4,2,3,1,0:T(2,128)}, u32[]{:S(2)}) copy-start(f32[1,1,2,3,20]{4,2,3,1,0:T(2,128)} %param.17) | copy-start | bytes 1444
  15.5 5.1 %copy-start = (f32[1,1,3,4096]{3,1,2,0:T(1,128)S(1)}, f32[1,1,3,4096]{3,1,2,0:T(1,128)}, u32[]{:S(2)}) copy-start(f32[1,1,3,4096]{3,1,2,0:T(1,128)} %param.22) | copy-start | bytes 147460
  20.5 0.8 %copy-start.1 = (f32[1,1,3,4096]{3,1,2,0:T(1,128)S(1)}, f32[1,1,3,4096]{3,1,2,0:T(1,128)}, u32[]{:S(2)}) copy-start(f32[1,1,3,4096]{3,1,2,0:T(1,128)} %param.23) | copy-start | bytes 147460

commit v4 on v3

--- a/solution.py
+++ b/solution.py
@@ -394,7 +394,7 @@
             dma((2,)),
         ],
         compiler_params=pltpu.CompilerParams(
-            collective_id=1, has_side_effects=True
+            collective_id=1, has_side_effects=True, vmem_limit_bytes=40 * 1024 * 1024
         ),
         name="merge",
     )(pay, coadd_sum, coadd_weight)

time: 36.7 us -> 34.5 us (0.940)
  Pallas kernels: 31.4 us -> 29.7 us
  local copies, waits for them, and re-layouts: 4.28 us -> 3.76 us
    pallas_call x1, Pallas kernels: 12.9 us -> 11.2 us  [shards(): pl.pallas_call(functools.partial(merge_kernel, n, skies, patches), out_sh...]
    unnamed x13 -> x15, local copies, waits for them, and re-layouts: 4.28 us -> 3.76 us
where the time goes in v4:
time: 34.5 us; the launch traced here: 34.2 us
  Pallas kernels  29.7 us (86%)
  local copies, waits for them, and re-layouts  3.76 us (11%)
  between operations  0.71 us (2%)
    pallas_call x1, Pallas kernels, shards(): pl.pallas_call(functools.partial(align_kernel, n, visits), out_shape=jax....  13.5 us
    pallas_call x1, Pallas kernels, shards(): pl.pallas_call(functools.partial(merge_kernel, n, skies, patches), out_sh...  11.2 us
    pallas_call x1, Pallas kernels, shards(): pl.pallas_call(functools.partial(match_kernel, patch_total, patches), out...  5.05 us
    unnamed x15, local copies, waits for them, and re-layouts  3.76 us

profile of v4, /device:TPU:0, one launch (start us, length us, event | category | flops | bytes accessed | tf_op | source)
XLA Modules:
  0.0 34.2 jit_solution(13484506970916190085)
XLA Ops:
  0.6 0.0 copy-start.4
  0.6 13.5 %align.1.strips_ref = bf16[8,2,64,128]{3,2,1,0:T(8,128)(2,1)} custom-call(s32[1,2]{1,0:T(1,128)} %offset_ref.1, bf16[1,1,128,512]{3,2,1,0:T(8,128)(2,1)} %template_ref.1), custom_call_target="tpu_custom_call" | custom-call | tf_op jit(solution)/shard_map/align/pallas_call | solution.py:330
  14.1 0.0 copy-done.4
  14.1 0.0 copy-start.3
  14.2 0.7 %copy.14.index_ref = s32[20,2]{1,0:T(8,128)} copy(s32[20,2]{0,1:T(2,128)S(1)} %copy-done.4) | data formatting | bytes 320 | tf_op args[4]
  14.8 0.0 copy-done.3
  14.8 0.6 %copy.15.coeff_ref = f32[1,1,2,3,20]{4,3,2,1,0:T(4,128)} copy(f32[1,1,2,3,20]{4,2,3,1,0:T(2,128)S(1)} %copy-done.3) | data formatting | bytes 960 | tf_op args[5]
  15.4 0.0 copy-start.1
  15.4 5.0 %match.1 = (f32[1,1,2,128,512]{4,3,2,1,0:T(8,128)}, bf16[24,2,32,128]{3,2,1,0:T(8,128)(2,1)}) custom-call(bf16[8,2,64,128]{3,2,1,0:T(8,128)(2,1)} %align.1.strips_ref, bf16[8,21]{1,0:T(8,128)(2,1)} %filters_ref.1, s32[20,2]{1,0:T(8,128)} %copy.14.index_ref, f32[1,1,2,3,20]{4,3,2,1,0:T(4,128)} %copy.15.coeff_ref, f32[1,1,2,128,512]{4,3,2,1,0:T(8,128)} %science_hbm.1, ...), custom_call_target="tpu_custom_call" | custom-call | tf_op jit(solution)/shard_map/match/pallas_call | solution.py:349
  20.5 0.0 copy-done.1
  20.5 0.0 copy-start.2
  20.5 0.7 %copy-done.2 = f32[1,1,3,4096]{3,1,2,0:T(1,128)S(1)} copy-done((f32[1,1,3,4096]{3,1,2,0:T(1,128)S(1)}, f32[1,1,3,4096]{3,1,2,0:T(1,128)}, u32[]{:S(2)}) %copy-start.2) | copy-done | bytes 49176
  21.3 0.0 copy-start
  21.3 1.0 %copy-done = bf16[24,2,32,128]{3,2,1,0:T(8,128)(2,1)S(1)} copy-done((bf16[24,2,32,128]{3,2,1,0:T(8,128)(2,1)S(1)}, bf16[24,2,32,128]{3,2,1,0:T(8,128)(2,1)}, u32[]{:S(2)}) %copy-start) | copy-done | bytes 393240
  22.3 11.2 %merge.1 = f32[1,1,3,4096]{3,2,1,0:T(4,128)S(1)} custom-call(bf16[24,2,32,128]{3,2,1,0:T(8,128)(2,1)S(1)} %copy-done, f32[1,1,3,4096]{3,2,1,0:T(4,128)S(1)} %copy.16.sum_ref, f32[1,1,3,4096]{3,2,1,0:T(4,128)S(1)} %copy.17.weight_ref), custom_call_target="tpu_custom_call" | custom-call | tf_op jit(solution)/shard_map/merge/pallas_call | solution.py:381
  33.5 0.7 %copy.18 = f32[1,1,3,4096]{3,1,2,0:T(1,128)} copy(f32[1,1,3,4096]{3,2,1,0:T(4,128)S(1)} %merge.1) | data formatting | bytes 98304
  (2 shorter events, 0.1 us)
Async XLA Ops:
  0.6 13.5 %copy-start.4 = (s32[20,2]{0,1:T(2,128)S(1)}, s32[20,2]{0,1:T(2,128)}, u32[]{:S(2)}) copy-start(s32[20,2]{0,1:T(2,128)} %param.16) | copy-start | bytes 484
  14.1 0.7 %copy-start.3 = (f32[1,1,2,3,20]{4,2,3,1,0:T(2,128)S(1)}, f32[1,1,2,3,20]{4,2,3,1,0:T(2,128)}, u32[]{:S(2)}) copy-start(f32[1,1,2,3,20]{4,2,3,1,0:T(2,128)} %param.17) | copy-start | bytes 1444
  15.4 5.1 %copy-start.1 = (f32[1,1,3,4096]{3,1,2,0:T(1,128)S(1)}, f32[1,1,3,4096]{3,1,2,0:T(1,128)}, u32[]{:S(2)}) copy-start(f32[1,1,3,4096]{3,1,2,0:T(1,128)} %param.22) | copy-start | bytes 147460
  20.5 0.8 %copy-start.2 = (f32[1,1,3,4096]{3,1,2,0:T(1,128)S(1)}, f32[1,1,3,4096]{3,1,2,0:T(1,128)}, u32[]{:S(2)}) copy-start(f32[1,1,3,4096]{3,1,2,0:T(1,128)} %param.23) | copy-start | bytes 147460
  21.3 1.0 %copy-start = (bf16[24,2,32,128]{3,2,1,0:T(8,128)(2,1)S(1)}, bf16[24,2,32,128]{3,2,1,0:T(8,128)(2,1)}, u32[]{:S(2)}) copy-start(bf16[24,2,32,128]{3,2,1,0:T(8,128)(2,1)} %get-tuple-element.5.pay_ref) | copy-start | bytes 1179652
